TPU v7x, 32 devices: a whole 2x2x4 slice. The times are simulated.
32 devices in a mesh: ctx: 8 (over z, y), head: 4 (over x, core).
Axes of the slice: x: 2, y: 2, z: 4, core: 2. Of those that a mesh axis runs over, the one named last changes fastest.
Arguments:
- queries: bfloat16 [8192, 64, 128], P('ctx', 'head'), may hold values from -8 to 8
- key_rows: bfloat16 [8192, 64, 128], P('ctx', 'head'), may hold values from -4 to 4
- value_rows: bfloat16 [8192, 64, 128], P('ctx', 'head'), may hold values from -12 to 12
- grad_normed: bfloat16 [8192, 64, 128], P('ctx', 'head'), may hold values from -6 to 6
- norm_gain: float32 [64, 128], P('head'), may hold values from 0.1 to 1.9
- document_starts: int32 [6], replicated, may hold values from 0 to 8064, as said below
Outputs:
- normed: bfloat16 [8192, 64, 128], P('ctx', 'head')
- grad_queries: bfloat16 [8192, 64, 128], P('ctx', 'head')
- grad_keys: bfloat16 [8192, 64, 128], P('ctx', 'head')
- grad_values: bfloat16 [8192, 64, 128], P('ctx', 'head')
- grad_gain: float32 [64, 128], P('head')
Inputs may be any that keep to these rules, and one draw needn't show every extreme that they name: `document_starts`: strictly increasing multiples of 128; the first is 0 and the last is 8064.
All inputs are finite; a program needn't handle non-finite values.
Results may differ from a plain program's by a relative error of at most 0.0057.
Values sent between devices are 32-bit elements; how exact they have to be, the bound alone decides.
No kernel may reach another device: no remote copies, remote signals or barrier semaphores. Data moves between devices by JAX's collectives and lax.ppermute only.
A program may use at most 192 MiB of HBM per device.

v0:
```python
import math

import jax
import jax.numpy as jnp
from jax import lax
from jax.sharding import PartitionSpec as P

HEADS = 64
HEAD_DIM = 128
TILE = 512


EPSILON = 1e-06


def token_documents(starts, positions):
    return jnp.sum((starts[None, :] <= positions[:, None]).astype(jnp.int32), axis=1) - 1


def local(queries, key_rows, value_rows, grad_normed, norm_gain, document_starts):
    shard_rows, local_heads, head_width = queries.shape
    tile_count = shard_rows // TILE
    shard_count = lax.axis_size("ctx")
    shard_index = lax.axis_index("ctx")
    feature_count = HEADS * HEAD_DIM
    first_row = shard_index * shard_rows
    positions = first_row + jnp.arange(shard_rows, dtype=jnp.int32)
    documents = token_documents(document_starts, positions).reshape(tile_count, TILE)
    tile_first = first_row + jnp.arange(tile_count, dtype=jnp.int32) * TILE
    prior_docs = token_documents(document_starts, tile_first - 1)
    last_docs = documents[:, -1]
    entering = (documents == prior_docs[:, None]).astype(jnp.float32)
    leaving = (documents == last_docs[:, None]).astype(jnp.float32)
    keep_flags = (last_docs == prior_docs).astype(jnp.float32)
    causal = jnp.arange(TILE)[:, None] >= jnp.arange(TILE)[None, :]
    within = (causal[None] & (documents[:, :, None] == documents[:, None, :])).astype(jnp.float32)[
        :, None
    ]
    enter_col = entering[:, :, None, None]
    leave_col = leaving[:, :, None, None]
    tiled_query = queries.reshape(tile_count, TILE, local_heads, head_width)
    tiled_key = key_rows.reshape(tile_count, TILE, local_heads, head_width)
    tiled_value = value_rows.reshape(tile_count, TILE, local_heads, head_width)
    scores = jnp.einsum(
        "cthd,cshd->chts", tiled_query, tiled_key, preferred_element_type=jnp.float32
    )
    attention = (scores * within).astype(jnp.bfloat16)
    intra_out = jnp.einsum(
        "chts,cshd->cthd", attention, tiled_value, preferred_element_type=jnp.float32
    )
    leave_keys = tiled_key * leave_col.astype(jnp.bfloat16)
    tile_states = jnp.einsum(
        "cthd,cthe->chde", leave_keys, tiled_value, preferred_element_type=jnp.float32
    )
    running = jnp.zeros_like(tile_states[0])
    local_entry = []
    for tile_number in range(tile_count):
        local_entry.append(running)
        running = tile_states[tile_number] + keep_flags[tile_number] * running
    reach_in = jnp.cumprod(jnp.concatenate([jnp.ones((1,), jnp.float32), keep_flags[:-1]]))
    reach_out = jnp.cumprod(jnp.concatenate([keep_flags[1:], jnp.ones((1,), jnp.float32)])[::-1])[
        ::-1
    ]
    source_shards = document_starts // shard_rows
    lowest = jnp.max(jnp.where(source_shards < shard_index, source_shards, 0))
    gathered = lax.all_gather(running[None], "ctx", axis=0, tiled=True)
    indices = jnp.arange(gathered.shape[0], dtype=jnp.int32)
    weights = ((indices >= lowest) & (indices < shard_index)).astype(jnp.float32)
    incoming = jnp.sum(weights[:, None, None, None] * gathered, axis=0)
    entry_states = jnp.stack(local_entry) + reach_in[:, None, None, None] * incoming[None]
    entry_bf = entry_states.astype(jnp.bfloat16)
    inter_out = jnp.einsum(
        "cthd,chde->cthe", tiled_query, entry_bf, preferred_element_type=jnp.float32
    )
    attended = intra_out + enter_col * inter_out
    upstream = grad_normed.reshape(tile_count, TILE, local_heads, head_width).astype(jnp.float32)
    weighted = upstream * norm_gain
    local_squares = jnp.sum(attended * attended, axis=(2, 3))
    local_cross = jnp.sum(weighted * attended, axis=(2, 3))
    squares, cross_sum = lax.psum((local_squares, local_cross), "head")
    inverse = 1.0 / jnp.sqrt(squares / feature_count + EPSILON)
    scaled = attended * inverse[:, :, None, None]
    normed = (scaled * norm_gain).astype(jnp.bfloat16)
    grad_att = (
        inverse[:, :, None, None] * weighted
        - attended * (inverse**3 * cross_sum / feature_count)[:, :, None, None]
    ).astype(jnp.bfloat16)
    gain_local = jnp.sum(upstream * scaled, axis=(0, 1))
    grad_gain = lax.psum(gain_local, "ctx") / math.sqrt(shard_rows * shard_count)
    grad_scores = (
        jnp.einsum("cthe,cshe->chts", grad_att, tiled_value, preferred_element_type=jnp.float32)
        * within
    ).astype(jnp.bfloat16)
    query_intra = jnp.einsum(
        "chts,cshd->cthd", grad_scores, tiled_key, preferred_element_type=jnp.float32
    )
    key_intra = jnp.einsum(
        "chts,cthd->cshd", grad_scores, tiled_query, preferred_element_type=jnp.float32
    )
    value_intra = jnp.einsum(
        "chts,cthe->cshe", attention, grad_att, preferred_element_type=jnp.float32
    )
    query_inter = jnp.einsum(
        "cthe,chde->cthd", grad_att, entry_bf, preferred_element_type=jnp.float32
    )
    grad_queries = (query_intra + enter_col * query_inter).astype(jnp.bfloat16)
    enter_queries = tiled_query * enter_col.astype(jnp.bfloat16)
    tile_grads = jnp.einsum(
        "cthd,cthe->chde", enter_queries, grad_att, preferred_element_type=jnp.float32
    )
    later_sum = jnp.zeros_like(tile_grads[0])
    local_exit = [later_sum] * tile_count
    for tile_number in reversed(range(tile_count)):
        local_exit[tile_number] = later_sum
        later_sum = tile_grads[tile_number] + keep_flags[tile_number] * later_sum
    highest = jnp.min(jnp.where(source_shards > shard_index, source_shards, shard_count - 1))
    gathered = lax.all_gather(later_sum[None], "ctx", axis=0, tiled=True)
    indices = jnp.arange(gathered.shape[0], dtype=jnp.int32)
    weights = ((indices > shard_index) & (indices <= highest)).astype(jnp.float32)
    outgoing = jnp.sum(weights[:, None, None, None] * gathered, axis=0)
    exit_states = jnp.stack(local_exit) + reach_out[:, None, None, None] * outgoing[None]
    exit_bf = exit_states.astype(jnp.bfloat16)
    key_inter = jnp.einsum(
        "cthe,chde->cthd", tiled_value, exit_bf, preferred_element_type=jnp.float32
    )
    value_inter = jnp.einsum(
        "cthd,chde->cthe", tiled_key, exit_bf, preferred_element_type=jnp.float32
    )
    grad_keys = (key_intra + leave_col * key_inter).astype(jnp.bfloat16)
    grad_values = (value_intra + leave_col * value_inter).astype(jnp.bfloat16)
    whole = (shard_rows, local_heads, head_width)
    return (
        normed.reshape(whole),
        grad_queries.reshape(whole),
        grad_keys.reshape(whole),
        grad_values.reshape(whole),
        grad_gain,
    )


def solution(mesh):
    in_specs = (
        P("ctx", "head", None),
        P("ctx", "head", None),
        P("ctx", "head", None),
        P("ctx", "head", None),
        P("head", None),
        P(),
    )
    out_specs = (
        P("ctx", "head", None),
        P("ctx", "head", None),
        P("ctx", "head", None),
        P("ctx", "head", None),
        P("head", None),
    )
    return jax.shard_map(local, mesh=mesh, in_specs=in_specs, out_specs=out_specs, check_vma=False)
```

profile of v0, /device:TPU:0, one launch (start us, length us, event | category | flops | bytes accessed | tf_op | source)
XLA Modules:
  0.0 364.4 jit_solution(12066071488426219159)
XLA Ops:
  9.7 7.5 %copy.122 = bf16[2,512,16,128]{1,3,2,0:T(8,128)(2,1)} copy(bf16[2,512,16,128]{3,2,1,0:T(8,128)(2,1)} %bitcast.55) | data formatting | bytes 8388608 | tf_op jit(solution)/shard_map/reshape | solution.py:42
  17.8 5.8 %fusion.5 = f32[2,16,128,128]{3,2,1,0:T(8,128)S(1)} fusion(bf16[2,512,16,128]{1,3,2,0:T(8,128)(2,1)} %copy.122, bf16[2,512,16,128]{3,2,1,0:T(8,128)(2,1)} %bitcast.49, bf16[2,512]{1,0:T(2,128)(2,1)S(1)} %get-tuple-element.15), kind=kOutput, calls=%fused_computation.19 | convolution fusion | flops 538968064 | bytes 10487808 | tf_op jit(solution)/shard_map/cthd,cthe->chde/dot_general | solution.py:52
  26.8 7.5 %copy.135 = bf16[2,512,16,128]{1,3,2,0:T(8,128)(2,1)} copy(bf16[2,512,16,128]{3,2,1,0:T(8,128)(2,1)} %bitcast.56) | data formatting | bytes 8388608 | tf_op jit(solution)/shard_map/reshape | solution.py:41
  37.0 6.6 %bitcast_convert_fusion = f32[2,512,16,128]{3,2,1,0:T(8,128)} fusion(bf16[1024,16,128]{2,1,0:T(8,128)(2,1)} %param.9), kind=kLoop, calls=%fused_computation.64 | loop fusion | flops 2097152 | bytes 12582912 | tf_op jit(solution)/shard_map/convert_element_type | solution.py:76
  43.6 10.4 %multiply_convert_fusion.1 = bf16[2,16,512,512]{3,2,1,0:T(8,128)(2,1)} fusion(bf16[2,512,16,128]{1,3,2,0:T(8,128)(2,1)S(1)} %copy-done, bf16[2,512,16,128]{1,3,2,0:T(8,128)(2,1)} %copy.122, f32[2,512,512]{2,1,0:T(8,128)S(1)} %and_convert_fusion), kind=kOutput, calls=%fused_computation.1 | convolution fusion | flops 2164260864 | bytes 27262976 | tf_op jit(solution)/shard_map/cthd,cshd->chts/dot_general | solution.py:44
  53.9 14.8 %fusion.10 = f32[2,16,512,128]{3,2,1,0:T(8,128)} fusion(bf16[2,16,512,512]{3,2,1,0:T(8,128)(2,1)} %multiply_convert_fusion.1, bf16[2,512,16,128]{3,2,1,0:T(8,128)(2,1)} %bitcast.50), kind=kOutput, calls=%fused_computation.24 | convolution fusion | flops 2147483648 | bytes 29360128 | tf_op jit(solution)/shard_map/chts,cshd->cthd/dot_general | solution.py:48
  68.7 84.9 %all-gather.3.cloned.1.call-done = f32[8,16,128,128]{3,2,1,0:T(8,128)} async-done(((f32[1,16,128,128]{3,2,1,0:T(8,128)}), f32[8,16,128,128]{3,2,1,0:T(8,128)}) %all-gather.3.cloned.1.call-update) | async-done | bytes 8388624 | tf_op jit(solution)/shard_map/all_gather | solution.py:66
  158.5 7.4 %multiply_reduce_fusion.3 = (f32[2,512]{1,0:T(2,128)S(1)}, f32[2,512,16,128]{3,1,2,0:T(8,128)}) fusion(bf16[2,512,16,128]{1,3,2,0:T(8,128)(2,1)S(1)} %copy-done.1, f32[1,16,128,128]{3,2,1,0:T(8,128)S(1)} %copy-done.8, f32[16,128,128]{2,1,0:T(8,128)S(1)} %multiply_reduce_fusion.4, f32[2]{0:T(128)S(1)} %bitcast.61, f32[2,512]{1,0:T(2,128)S(1)} %get-tuple-element.20, ...), kind=kOutput, calls=%fused_computation.13 | convolution fusion | flops 546831360 | bytes 23076872 | tf_op jit(solution)/shard_map/cthd,chde->cthe/dot_general | solution.py:72
  165.9 6.4 %psum.21 = f32[2,512]{1,0:T(2,128)S(1)} all-reduce(f32[2,512]{1,0:T(2,128)S(1)} %get-tuple-element.23), channel_id=1, replica_groups=mesh['ctx'=8,'head'=4] {'head'}, use_global_device_ids=true, to_apply=%region_6.7 | all-reduce | flops 1024 | bytes 8192 | tf_op jit(solution)/shard_map/psum | solution.py:80
  172.3 9.3 %multiply_reduce_fusion = (f32[16,128]{1,0:T(8,128)S(1)}, f32[2,512]{1,0:T(2,128)S(1)}) fusion(f32[2,512,16,128]{3,2,1,0:T(8,128)} %bitcast_convert_fusion, f32[2,512,16,128]{3,1,2,0:T(8,128)} %get-tuple-element.24, f32[2,512]{1,0:T(2,128)S(1)} %add_rsqrt_fusion, f32[16,128]{1,0:T(8,128)S(1)} %copy-done.10), kind=kLoop, calls=%fused_computation.7 | loop fusion | flops 12579840 | bytes 16801792 | tf_op jit(solution)/shard_map/reduce_sum | solution.py:88
  181.6 6.1 %psum.22 = f32[2,512]{1,0:T(2,128)S(1)} all-reduce(f32[2,512]{1,0:T(2,128)S(1)} %get-tuple-element.6), channel_id=1, replica_groups=mesh['ctx'=8,'head'=4] {'head'}, use_global_device_ids=true, to_apply=%region_8.9 | all-reduce | flops 1024 | bytes 8192 | tf_op jit(solution)/shard_map/psum | solution.py:80
  187.7 9.7 %subtract_convert_fusion = (bf16[2,512,16,128]{3,1,2,0:T(8,128)(2,1)S(1)}, bf16[2,512,16,128]{3,1,2,0:T(8,128)(2,1)}) fusion(f32[2,512,16,128]{3,1,2,0:T(8,128)} %get-tuple-element.24, f32[2,512,16,128]{3,2,1,0:T(8,128)} %bitcast_convert_fusion, f32[2,512]{1,0:T(2,128)S(1)} %fusion.15, f32[16,128]{1,0:T(8,128)S(1)} %copy-done.10, f32[2,512]{1,0:T(2,128)S(1)} %add_rsqrt_fusion), kind=kLoop, calls=%fused_computation.10 | loop fusion | flops 16777216 | bytes 25182208 | tf_op jit(solution)/shard_map/convert_element_type | solution.py:87
  203.3 6.9 %copy.127 = bf16[2,512,16,128]{3,2,1,0:T(8,128)(2,1)} copy(bf16[2,512,16,128]{3,1,2,0:T(8,128)(2,1)} %get-tuple-element.18) | data formatting | bytes 8388608 | tf_op jit(solution)/shard_map/convert_element_type | solution.py:83
  210.2 11.7 %multiply_convert_fusion = bf16[2,16,512,512]{3,2,1,0:T(8,128)(2,1)} fusion(bf16[2,512,16,128]{3,1,2,0:T(8,128)(2,1)} %copy-done.3, f32[2,512,512]{2,1,0:T(8,128)S(1)} %and_convert_fusion, bf16[2,512,16,128]{3,2,1,0:T(8,128)(2,1)} %bitcast.51), kind=kOutput, calls=%fused_computation | convolution fusion | flops 2164260864 | bytes 27262976 | tf_op jit(solution)/shard_map/cthe,cshe->chts/dot_general | solution.py:91
  221.9 14.9 %fusion.22 = f32[2,16,512,128]{3,2,1,0:T(8,128)} fusion(bf16[2,16,512,512]{3,2,1,0:T(8,128)(2,1)} %multiply_convert_fusion, bf16[2,512,16,128]{1,3,2,0:T(8,128)(2,1)} %copy.122), kind=kOutput, calls=%fused_computation.68 | convolution fusion | flops 2147483648 | bytes 29360128 | tf_op jit(solution)/shard_map/chts,cshd->cthd/dot_general | solution.py:94
  236.8 6.0 %fusion.1 = bf16[2,512,16,128]{3,1,2,0:T(8,128)(2,1)S(1)} fusion(f32[2,16,512,128]{3,2,1,0:T(8,128)} %fusion.22, f32[2,512]{1,0:T(2,128)S(1)} %get-tuple-element.20, bf16[2,512,16,128]{3,1,2,0:T(8,128)(2,1)} %copy-done.3, f32[1,16,128,128]{3,2,1,0:T(8,128)S(1)} %copy-done.9, f32[16,128,128]{2,1,0:T(8,128)S(1)} %copy-done.7, f32[2]{0:T(128)S(1)} %bitcast.62), kind=kOutput, calls=%fused_computation.5 | convolution fusion | flops 544735232 | bytes 18878472 | tf_op jit(solution)/shard_map/cthe,chde->cthd/dot_general | solution.py:103
  247.6 20.5 %psum.23 = f32[16,128]{1,0:T(8,128)S(1)} all-reduce(f32[16,128]{1,0:T(8,128)S(1)} %get-tuple-element.5), channel_id=1, replica_groups=mesh['ctx'=8,'head'=4] {'ctx'}, use_global_device_ids=true, to_apply=%region_13.14 | all-reduce | flops 2048 | bytes 16384 | tf_op jit(solution)/shard_map/psum | solution.py:89
  268.7 11.6 %fusion.24 = f32[2,16,128,512]{2,3,1,0:T(8,128)} fusion(bf16[2,512,16,128]{3,1,2,0:T(8,128)(2,1)} %copy-done.3, bf16[2,16,512,512]{3,2,1,0:T(8,128)(2,1)} %multiply_convert_fusion.1), kind=kOutput, calls=%fused_computation.70 | convolution fusion | flops 2147483648 | bytes 29360128 | tf_op jit(solution)/shard_map/chts,cthe->cshe/dot_general | solution.py:100
  280.3 11.4 %fusion.23 = f32[2,16,512,128]{3,2,1,0:T(8,128)} fusion(bf16[2,16,512,512]{3,2,1,0:T(8,128)(2,1)} %multiply_convert_fusion, bf16[2,512,16,128]{1,3,2,0:T(8,128)(2,1)} %copy.135), kind=kOutput, calls=%fused_computation.69 | convolution fusion | flops 2147483648 | bytes 29360128 | tf_op jit(solution)/shard_map/chts,cthd->cshd/dot_general | solution.py:97
  291.7 33.6 %all-gather.5.cloned.1.call-done = f32[8,16,128,128]{3,2,1,0:T(8,128)} async-done(((f32[1,16,128,128]{3,2,1,0:T(8,128)}), f32[8,16,128,128]{3,2,1,0:T(8,128)}) %all-gather.5.cloned.1.call-update) | async-done | bytes 8388624 | tf_op jit(solution)/shard_map/all_gather | solution.py:117
  330.0 8.0 %fusion.2 = bf16[2,512,16,128]{3,1,2,0:T(8,128)(2,1)} fusion(f32[2,16,128,512]{2,3,1,0:T(8,128)} %fusion.24, f32[2,512]{1,0:T(2,128)S(1)} %get-tuple-element.16, bf16[2,512,16,128]{1,3,2,0:T(8,128)(2,1)S(1)} %copy-done.4, f32[1,16,128,128]{3,2,1,0:T(8,128)} %get-tuple-element.10, f32[16,128,128]{2,1,0:T(8,128)S(1)} %multiply_reduce_fusion.1, f32[2]{0:T(128)S(1)} %rev.7), kind=kOutput, calls=%fused_computation.16 | convolution fusion | flops 544735232 | bytes 18878472 | tf_op jit(solution)/shard_map/cthd,chde->cthe/dot_general | solution.py:126
  338.0 7.0 %copy.144 = bf16[2,512,16,128]{3,2,1,0:T(8,128)(2,1)} copy(bf16[2,512,16,128]{3,1,2,0:T(8,128)(2,1)} %fusion.2) | data formatting | bytes 8388608 | tf_op jit(solution)/shard_map/convert_element_type | solution.py:130
  345.1 5.3 %fusion = bf16[2,512,16,128]{3,1,2,0:T(8,128)(2,1)} fusion(f32[2,16,512,128]{3,2,1,0:T(8,128)S(1)} %bitcast.54, f32[2,512]{1,0:T(2,128)S(1)} %get-tuple-element.16, bf16[2,512,16,128]{3,2,1,0:T(8,128)(2,1)S(1)} %bitcast.52, f32[1,16,128,128]{3,2,1,0:T(8,128)} %get-tuple-element.10, f32[16,128,128]{2,1,0:T(8,128)S(1)} %multiply_reduce_fusion.1, f32[2]{0:T(128)S(1)} %rev.7), kind=kOutput, calls=%fused_computation.3 | convolution fusion | flops 544735232 | bytes 18878472 | tf_op jit(solution)/shard_map/cthe,chde->cthd/dot_general | solution.py:123
  350.4 6.9 %copy.138 = bf16[2,512,16,128]{3,2,1,0:T(8,128)(2,1)} copy(bf16[2,512,16,128]{3,1,2,0:T(8,128)(2,1)} %fusion) | data formatting | bytes 8388608 | tf_op jit(solution)/shard_map/convert_element_type | solution.py:129
  (64 shorter events, 28.5 us)
Async XLA Ops:
  7.2 146.5 %all-gather.3.cloned.1.call-start = ((), (), s32[]{:S(2)}) async-start(), calls=%async_computation | async-start | bytes 9437184 | tf_op jit(solution)/shard_map/all_gather | solution.py:66
  25.8 299.5 %all-gather.5.cloned.1.call-start = ((), (), s32[]{:S(2)}) async-start(), calls=%async_computation.1 | async-start | bytes 9437184 | tf_op jit(solution)/shard_map/all_gather | solution.py:117
  26.7 8.4 %copy-start.11 = (s32[6]{0:T(128)S(1)}, s32[6]{0:T(128)}, u32[]{:S(2)}) copy-start(s32[6]{0:T(128)} %param.11) | copy-start | bytes 76
  37.0 6.6 %copy-start = (bf16[2,512,16,128]{1,3,2,0:T(8,128)(2,1)S(1)}, bf16[2,512,16,128]{1,3,2,0:T(8,128)(2,1)}, u32[]{:S(2)}) copy-start(bf16[2,512,16,128]{1,3,2,0:T(8,128)(2,1)} %copy.135) | copy-start | bytes 12582916
  153.6 4.8 %copy-start.1 = (bf16[2,512,16,128]{1,3,2,0:T(8,128)(2,1)S(1)}, bf16[2,512,16,128]{1,3,2,0:T(8,128)(2,1)}, u32[]{:S(2)}) copy-start(bf16[2,512,16,128]{1,3,2,0:T(8,128)(2,1)} %copy.135) | copy-start | bytes 12582916
  153.6 4.9 %copy-start.8 = (f32[1,16,128,128]{3,2,1,0:T(8,128)S(1)}, f32[1,16,128,128]{3,2,1,0:T(8,128)}, u32[]{:S(2)}) copy-start(f32[1,16,128,128]{3,2,1,0:T(8,128)} %get-tuple-element.14) | copy-start | bytes 3145732
  158.4 7.5 %copy-start.6 = (f32[16,128,128]{2,1,0:T(8,128)}, f32[16,128,128]{2,1,0:T(8,128)S(1)}, u32[]{:S(2)}) copy-start(f32[16,128,128]{2,1,0:T(8,128)S(1)} %multiply_reduce_fusion.4) | copy-start | bytes 3145732
  158.5 13.8 %copy-start.10 = (f32[16,128]{1,0:T(8,128)S(1)}, f32[16,128]{1,0:T(8,128)}, u32[]{:S(2)}) copy-start(f32[16,128]{1,0:T(8,128)} %param.10) | copy-start | bytes 24580
  187.7 9.7 %copy-start.2 = (bf16[2,512,16,128]{1,3,2,0:T(8,128)(2,1)S(1)}, bf16[2,512,16,128]{1,3,2,0:T(8,128)(2,1)}, u32[]{:S(2)}) copy-start(bf16[2,512,16,128]{1,3,2,0:T(8,128)(2,1)} %copy.135) | copy-start | bytes 12582916
  197.4 2.0 copy-start.3
  221.8 15.0 %copy-start.7 = (f32[16,128,128]{2,1,0:T(8,128)S(1)}, f32[16,128,128]{2,1,0:T(8,128)}, u32[]{:S(2)}) copy-start(f32[16,128,128]{2,1,0:T(8,128)} %copy-done.6) | copy-start | bytes 3145732
  221.9 14.9 %copy-start.9 = (f32[1,16,128,128]{3,2,1,0:T(8,128)S(1)}, f32[1,16,128,128]{3,2,1,0:T(8,128)}, u32[]{:S(2)}) copy-start(f32[1,16,128,128]{3,2,1,0:T(8,128)} %get-tuple-element.14) | copy-start | bytes 3145732
  325.3 4.7 %copy-start.4 = (bf16[2,512,16,128]{1,3,2,0:T(8,128)(2,1)S(1)}, bf16[2,512,16,128]{1,3,2,0:T(8,128)(2,1)}, u32[]{:S(2)}) copy-start(bf16[2,512,16,128]{1,3,2,0:T(8,128)(2,1)} %copy.122) | copy-start | bytes 12582916
  325.3 19.8 %slice-start = ((s8[8388608]{0:T(1024)(128)(4,1)}), s8[4194304]{0:T(1024)(128)(4,1)S(1)}, s32[]{:S(2)}) async-start(s8[8388608]{0:T(1024)(128)(4,1)} %bitcast.53), calls=%async_computation.2 | async-start | bytes 8388608
  330.0 15.0 %slice-start.1 = ((s8[8388608]{0:T(1024)(128)(4,1)}), s8[4194304]{0:T(1024)(128)(4,1)S(1)}, s32[]{:S(2)}) async-start(s8[8388608]{0:T(1024)(128)(4,1)} %bitcast.53), calls=%async_computation.3 | async-start | bytes 8388608
  338.0 7.1 %copy-start.5 = (bf16[1024,16,128]{2,1,0:T(8,128)(2,1)S(1)}, bf16[1024,16,128]{2,1,0:T(8,128)(2,1)}, u32[]{:S(2)}) copy-start(bf16[1024,16,128]{2,1,0:T(8,128)(2,1)} %param.8) | copy-start | bytes 12582916
Sparse Core Ops, SparseCore 0:
  25.9 127.6 all-gather.2
  201.7 123.5 all-gather.4
where the time goes:
time: 368 us; the launch traced here: 364 us
  waiting for transfers between devices  119 us (32%)
  matrix products  108 us (29%)
  other arithmetic  45.8 us (12%)
  local copies, waits for them, and re-layouts  42.4 us (12%)
  blocking collectives  33 us (9%)
  between operations  15.8 us (4%)
    all_gather x1, waiting for transfers between devices, local(): gathered = lax.all_gather(running[None], 'ctx', axis=0, tiled=True)  84.9 us
    all_gather x1, waiting for transfers between devices, local(): gathered = lax.all_gather(later_sum[None], 'ctx', axis=0, tiled=True)  33.6 us
    psum x1, blocking collectives, local(): lax.psum(gain_local, 'ctx') / math.sqrt(shard_rows * shard_count)  20.5 us
    dot_general x1, matrix products, local(): jnp.einsum('chts,cshd->cthd', grad_scores, tiled_key, preferred_element_t...  14.9 us
    dot_general x1, matrix products, local(): jnp.einsum('chts,cshd->cthd', attention, tiled_value, preferred_element_t...  14.8 us
    psum x2, blocking collectives, local(): squares, cross_sum = lax.psum((local_squares, local_cross), 'head')  12.5 us
    dot_general x1, matrix products, local(): jnp.einsum('cthe,cshe->chts', grad_att, tiled_value, preferred_element_ty...  11.7 us
    dot_general x1, matrix products, local(): jnp.einsum('chts,cthe->cshe', attention, grad_att, preferred_element_type...  11.6 us
  transfers between devices with their start and end apart: 2, of which 2 were waited for; matrix products, arithmetic and copies ran while one was open for 31% of the time, Pallas kernels for 0%

commit v1 on v0

v1 whole, which is shorter than its diff:
```python
import functools
import math

import jax
import jax.numpy as jnp
from jax import lax
from jax.experimental import pallas as pl
from jax.experimental.pallas import tpu as pltpu
from jax.sharding import PartitionSpec as P

CHUNK = 256
LANES = 128
EPSILON = 1e-06
FAR = 2**30
VMEM_LIMIT = 56 * 1024 * 1024

F32 = jnp.float32
BF16 = jnp.bfloat16


def dot_nn(a, b):
    return lax.dot_general(a, b, (((1,), (0,)), ((), ())), preferred_element_type=F32)


def dot_nt(a, b):
    return lax.dot_general(a, b, (((1,), (1,)), ((), ())), preferred_element_type=F32)


def dot_tn(a, b):
    return lax.dot_general(a, b, (((0,), (0,)), ((), ())), preferred_element_type=F32)


def first_start_from(starts, row):
    best = jnp.int32(FAR)
    for i in range(starts.shape[0]):
        best = jnp.minimum(best, jnp.where(starts[i] >= row, starts[i], FAR))
    return best


def last_start_to(starts, row):
    best = jnp.int32(0)
    for i in range(starts.shape[0]):
        best = jnp.maximum(best, jnp.where(starts[i] <= row, starts[i], 0))
    return best


def token_rows(first, shape, axis):
    return first + lax.broadcasted_iota(jnp.int32, shape, axis)


def within_mask(starts, first, axis):
    shape = (CHUNK, CHUNK)
    t = token_rows(first, shape, axis)
    s = token_rows(first, shape, 1 - axis)
    begin = jnp.zeros(shape, jnp.int32)
    for i in range(starts.shape[0]):
        begin = jnp.maximum(begin, jnp.where(starts[i] <= t, starts[i], 0))
    return jnp.where((s <= t) & (s >= begin), 1.0, 0.0).astype(BF16)


def before_mask(first, bound, dtype):
    return jnp.where(token_rows(first, (CHUNK, LANES), 0) < bound, 1.0, 0.0).astype(dtype)


def from_mask(first, bound, dtype):
    return jnp.where(token_rows(first, (CHUNK, LANES), 0) >= bound, 1.0, 0.0).astype(dtype)


def own_head(base, j, heads):
    return lax.rem(j + base[1] * (heads // 2), heads)


def spread(scratch, block):
    scratch[...] = block[...].astype(F32).reshape(scratch.shape)


def gather_rows(scratch, head, heads):
    return scratch[pl.ds(head, CHUNK, heads), :]


def state_kernel(starts, base, k_ref, v_ref, o0, o1, o2, o3, k_rows, v_rows, total):
    heads = k_ref.shape[1]
    step, steps = pl.program_id(0), pl.num_programs(0)
    first = base[0] + step * CHUNK
    bound = last_start_to(starts, base[0] + steps * CHUNK - 1)

    @pl.when(step == 0)
    def _():
        total[...] = jnp.zeros_like(total)

    @pl.when(bound < first + CHUNK)
    def _():
        spread(k_rows, k_ref)
        spread(v_rows, v_ref)
        leave = from_mask(first, bound, F32)

        def body(j, carry):
            head = own_head(base, j, heads)
            key = (gather_rows(k_rows, head, heads) * leave).astype(BF16)
            value = gather_rows(v_rows, head, heads).astype(BF16)
            total[j] += dot_tn(key, value)
            return carry

        lax.fori_loop(0, heads, body, 0, unroll=4)

    @pl.when(step == steps - 1)
    def _():
        part = heads // 4
        for i, out in enumerate((o0, o1, o2, o3)):
            out[...] = total[i * part : (i + 1) * part]


def turn_kernel(base, *refs):
    count = len(refs) // 3
    ins, outs, rows = refs[:count], refs[count : 2 * count], refs[2 * count :]
    heads = ins[0].shape[1]
    for source, out, scratch in zip(ins, outs, rows):
        spread(scratch, source)

        def body(j, carry, out=out, scratch=scratch):
            out[j] = gather_rows(scratch, own_head(base, j, heads), heads).astype(BF16)
            return carry

        lax.fori_loop(0, heads, body, 0, unroll=4)


def local_kernel(starts, base, q_ref, k_ref, v_ref, att_ref, entry_ref, state, mask, enter, leave):
    heads = q_ref.shape[0]
    step = pl.program_id(0)
    first = base[0] + step * CHUNK
    enter_end = first_start_from(starts, first)
    leave_start = last_start_to(starts, first + CHUNK - 1)
    keep = jnp.where(enter_end >= first + CHUNK, 1.0, 0.0).astype(F32)

    @pl.when(step == 0)
    def _():
        state[...] = jnp.zeros_like(state)

    mask[...] = within_mask(starts, first, 0)
    enter[...] = before_mask(first, enter_end, BF16)
    leave[...] = from_mask(first, leave_start, BF16)

    def body(j, carry):
        query, key, value = q_ref[j], k_ref[j], v_ref[j]
        entry = state[j].astype(BF16)
        entry_ref[0, j] = entry
        scores = dot_nt(query, key).astype(BF16) * mask[...]
        att_ref[j] = (dot_nn(scores, value) + dot_nn(query * enter[...], entry)).astype(att_ref.dtype)
        state[j] = keep * state[j] + dot_tn(key * leave[...], value)
        return carry

    lax.fori_loop(0, heads, body, 0, unroll=2)


def load_states(parts, held):
    part = parts[0].shape[0]
    for i, ref in enumerate(parts):
        held[i * part : (i + 1) * part] = ref[...].astype(held.dtype)


def eye():
    shape = (LANES, LANES)
    return lax.broadcasted_iota(jnp.int32, shape, 0) == lax.broadcasted_iota(jnp.int32, shape, 1)


def column_of(row):
    return jnp.sum(jnp.where(eye(), row, 0.0), axis=1, keepdims=True)


def row_of(column):
    return jnp.sum(jnp.where(eye(), column, 0.0), axis=0, keepdims=True)


def sums_kernel(starts, base, q_ref, att_ref, g_ref, gain, r0, r1, r2, r3, sums, held, squares, cross, enter):
    heads = q_ref.shape[0]
    step, steps = pl.program_id(0), pl.num_programs(0)
    first = base[0] + step * CHUNK

    @pl.when(step == 0)
    def _():
        load_states((r0, r1, r2, r3), held)

    enter[...] = before_mask(first, first_start_from(starts, base[0]), BF16)
    squares[...] = jnp.zeros_like(squares)
    cross[...] = jnp.zeros_like(cross)

    def body(j, carry):
        head = own_head(base, j, heads)
        att = att_ref[j].astype(F32) + dot_nn(q_ref[j] * enter[...], held[j])
        weighted = g_ref[j].astype(F32) * gain[pl.ds(head, 1), :]
        squares[...] += att * att
        cross[...] += weighted * att
        return carry

    lax.fori_loop(0, heads, body, 0, unroll=2)
    blocks = CHUNK // LANES
    for i in range(blocks):
        rows = slice(i * LANES, (i + 1) * LANES)
        place = step * blocks + i
        sums[pl.ds(place, 1), :] = row_of(jnp.sum(squares[rows, :], axis=1, keepdims=True))
        sums[pl.ds(steps * blocks + place, 1), :] = row_of(
            jnp.sum(cross[rows, :], axis=1, keepdims=True)
        )


def norm_columns(sums, step, steps, features, inverse, factor):
    blocks = CHUNK // LANES
    for i in range(blocks):
        rows = slice(i * LANES, (i + 1) * LANES)
        place = step * blocks + i
        square = sums[pl.ds(place, 1), :]
        cross = sums[pl.ds(steps * blocks + place, 1), :]
        inv = 1.0 / jnp.sqrt(square / features + EPSILON)
        fac = inv * inv * inv * cross / features
        inverse[rows, :] = jnp.broadcast_to(column_of(inv), (LANES, LANES))
        factor[rows, :] = jnp.broadcast_to(column_of(fac), (LANES, LANES))


def exit_kernel(
    features, starts, base, q_ref, att_ref, g_ref, gain, sums, r0, r1, r2, r3,
    o0, o1, o2, o3, held, inverse, factor, enter, total,
):
    heads = q_ref.shape[0]
    step, steps = pl.program_id(0), pl.num_programs(0)
    first = base[0] + step * CHUNK
    bound = first_start_from(starts, base[0])

    @pl.when(step == 0)
    def _():
        load_states((r0, r1, r2, r3), held)
        total[...] = jnp.zeros_like(total)

    @pl.when(bound > first)
    def _():
        norm_columns(sums, step, steps, features, inverse, factor)
        enter[...] = before_mask(first, bound, BF16)

        def body(j, carry):
            head = own_head(base, j, heads)
            query = q_ref[j] * enter[...]
            att = att_ref[j].astype(F32) + dot_nn(query, held[j])
            weighted = g_ref[j].astype(F32) * gain[pl.ds(head, 1), :]
            grad = (inverse[...] * weighted - att * factor[...]).astype(BF16)
            total[j] += dot_tn(query, grad)
            return carry

        lax.fori_loop(0, heads, body, 0, unroll=2)

    @pl.when(step == steps - 1)
    def _():
        part = heads // 4
        for i, out in enumerate((o0, o1, o2, o3)):
            out[...] = total[i * part : (i + 1) * part]


def query_kernel(
    features, starts, base, q_ref, k_ref, v_ref, att_ref, g_ref, entry_ref, gain, sums, r0, r1, r2, r3,
    normed, grad_q, grad_att, gain_sum,
    held, inverse, factor, enter, enter_all, mask, norm_rows, grad_rows, gain_total,
):
    heads = q_ref.shape[0]
    step, steps = pl.program_id(0), pl.num_programs(0)
    first = base[0] + step * CHUNK
    bound = first_start_from(starts, base[0])
    reach = jnp.where(bound >= first, 1.0, 0.0).astype(F32)

    @pl.when(step == 0)
    def _():
        load_states((r0, r1, r2, r3), held)
        gain_total[...] = jnp.zeros_like(gain_total)

    norm_columns(sums, step, steps, features, inverse, factor)
    enter_all[...] = before_mask(first, bound, BF16)
    enter[...] = before_mask(first, first_start_from(starts, first), F32)
    mask[...] = within_mask(starts, first, 0)

    def body(j, carry):
        head = own_head(base, j, heads)
        scale = gain[pl.ds(head, 1), :]
        state = held[j]
        att = att_ref[j].astype(F32) + dot_nn(q_ref[j] * enter_all[...], state.astype(BF16))
        upstream = g_ref[j].astype(F32)
        scaled = att * inverse[...]
        norm_rows[pl.ds(head, CHUNK, heads), :] = scaled * scale
        gain_total[pl.ds(head, 1), :] += jnp.sum(upstream * scaled, axis=0, keepdims=True)
        grad = (inverse[...] * (upstream * scale) - att * factor[...]).astype(BF16)
        grad_att[j] = grad
        entry = (entry_ref[0, j].astype(F32) + reach * state).astype(BF16)
        scores = dot_nt(grad, v_ref[j]).astype(BF16) * mask[...]
        grad_rows[pl.ds(head, CHUNK, heads), :] = dot_nn(scores, k_ref[j]) + enter[...] * dot_nt(grad, entry)
        return carry

    lax.fori_loop(0, heads, body, 0, unroll=2)
    normed[...] = norm_rows[...].reshape(normed.shape).astype(BF16)
    grad_q[...] = grad_rows[...].reshape(grad_q.shape).astype(BF16)

    @pl.when(step == steps - 1)
    def _():
        gain_sum[...] = gain_total[...]


def key_kernel(
    starts, base, q_ref, k_ref, v_ref, grad_ref, grad_k, grad_v, state, mask, enter, leave
):
    heads = q_ref.shape[0]
    step, steps = pl.program_id(0), pl.num_programs(0)
    first = base[0] + (steps - 1 - step) * CHUNK
    enter_end = first_start_from(starts, first)
    leave_start = last_start_to(starts, first + CHUNK - 1)
    keep = jnp.where(enter_end >= first + CHUNK, 1.0, 0.0).astype(F32)

    @pl.when(step == 0)
    def _():
        state[...] = jnp.zeros_like(state)

    mask[...] = within_mask(starts, first, 1)
    enter[...] = before_mask(first, enter_end, BF16)
    leave[...] = from_mask(first, leave_start, BF16)

    def body(j, carry):
        query, key, value, grad = q_ref[j], k_ref[j], v_ref[j], grad_ref[j]
        exits = state[j].astype(BF16)
        scores = dot_nt(key, query).astype(BF16) * mask[...]
        grad_v[j] = (dot_nn(scores, grad) + dot_nn(key * leave[...], exits)).astype(grad_v.dtype)
        scores = dot_nt(value, grad).astype(BF16) * mask[...]
        grad_k[j] = (dot_nn(scores, query) + dot_nt(value * leave[...], exits)).astype(grad_k.dtype)
        state[j] = keep * state[j] + dot_tn(query * enter[...], grad)
        return carry

    lax.fori_loop(0, heads, body, 0, unroll=2)


def last_kernel(
    starts, base, k_ref, v_ref, gk_ref, gv_ref, z0, z1, z2, z3, grad_k, grad_v, held, leave, k_rows, v_rows
):
    heads = k_ref.shape[0]
    step, steps = pl.program_id(0), pl.num_programs(0)
    first = base[0] + step * CHUNK

    @pl.when(step == 0)
    def _():
        load_states((z0, z1, z2, z3), held)

    leave[...] = from_mask(first, last_start_to(starts, base[0] + steps * CHUNK - 1), BF16)

    def body(j, carry):
        head = own_head(base, j, heads)
        exits = held[j]
        k_rows[pl.ds(head, CHUNK, heads), :] = gk_ref[j].astype(F32) + dot_nt(v_ref[j] * leave[...], exits)
        v_rows[pl.ds(head, CHUNK, heads), :] = gv_ref[j].astype(F32) + dot_nn(k_ref[j] * leave[...], exits)
        return carry

    lax.fori_loop(0, heads, body, 0, unroll=2)
    grad_k[...] = k_rows[...].reshape(grad_k.shape).astype(BF16)
    grad_v[...] = v_rows[...].reshape(grad_v.shape).astype(BF16)


SMEM = pl.BlockSpec(memory_space=pltpu.SMEM)


def params(limit=VMEM_LIMIT):
    return pltpu.CompilerParams(dimension_semantics=("arbitrary",), vmem_limit_bytes=limit)


def whole(shape):
    return pl.BlockSpec(shape, lambda c: (0,) * len(shape))


def pair_scan(parts, backward, shard, shards, keeps, hops):
    half = len(parts) // 2
    side = lax.rem(shard, 2)
    swap = [(i, i ^ 1) for i in range(shards)]
    groups = shards // 2
    if backward:
        step = [(i, i - 2) for i in range(2, shards)]
        lead = side == 1
        lead_keep, other_keep = keeps[shard | 1], keeps[shard - side]
    else:
        step = [(i, i + 2) for i in range(shards - 2)]
        lead = side == 0
        lead_keep, other_keep = keeps[shard - side], keeps[shard | 1]
    own_out, send_out = [], []
    arrived = [lax.ppermute(p, "ctx", swap) for p in parts[half:]]
    for mine, theirs in zip(parts[:half], arrived):
        first = jnp.where(lead, mine, theirs)
        second = jnp.where(lead, theirs, mine)
        pair = second + other_keep * first
        running = pair
        incoming = None
        for hop in range(hops):
            incoming = lax.ppermute(running, "ctx", step)
            if hop + 1 < hops:
                running = pair + (other_keep * lead_keep) * incoming
        later = first + lead_keep * incoming
        own_out.append(jnp.where(lead, incoming, later))
        send_out.append(jnp.where(lead, later, incoming))
    got = [lax.ppermute(p, "ctx", swap) for p in send_out]
    return own_out + got


def sum_over(x, axis):
    size = lax.axis_size(axis)
    if size & (size - 1):
        return lax.psum(x, axis)
    distance = 1
    while distance < size:
        x = x + lax.ppermute(x, axis, [(i, i ^ distance) for i in range(size)])
        distance *= 2
    return x


def local(queries, key_rows, value_rows, grad_normed, norm_gain, document_starts):
    rows, heads, width = queries.shape
    shards = lax.axis_size("ctx")
    shard = lax.axis_index("ctx")
    features = heads * lax.axis_size("head") * width
    steps = rows // CHUNK
    part = heads // 4
    base = jnp.stack([shard * rows, lax.rem(shard, 2)]).astype(jnp.int32)
    edges = jnp.arange(shards, dtype=jnp.int32)[:, None] * rows
    inside = (document_starts[None, :] >= edges) & (document_starts[None, :] < edges + rows)
    keeps = 1.0 - jnp.any(inside, axis=1).astype(F32)

    grid = (steps,)
    native = pl.BlockSpec((CHUNK, heads, width), lambda c: (c, 0, 0))
    major = pl.BlockSpec((heads, CHUNK, width), lambda c: (0, c, 0))
    major_back = pl.BlockSpec((heads, CHUNK, width), lambda c: (0, steps - 1 - c, 0))
    state_part = whole((part, width, width))
    gain_spec = whole((heads, width))
    native_shape = jax.ShapeDtypeStruct((rows, heads, width), BF16)
    major_shape = jax.ShapeDtypeStruct((heads, rows, width), BF16)
    part_shape = jax.ShapeDtypeStruct((part, width, width), F32)
    flat_rows = pltpu.VMEM((CHUNK * heads, width), F32)
    held_bf = pltpu.VMEM((heads, width, width), BF16)
    held_f = pltpu.VMEM((heads, width, width), F32)
    token_bf = pltpu.VMEM((CHUNK, width), BF16)
    token_f = pltpu.VMEM((CHUNK, width), F32)
    mask_bf = pltpu.VMEM((CHUNK, CHUNK), BF16)
    sum_rows = 2 * rows // LANES
    sums_spec = whole((sum_rows, LANES))

    states = pl.pallas_call(
        state_kernel,
        grid=grid,
        in_specs=[SMEM, SMEM, native, native],
        out_specs=[state_part] * 4,
        out_shape=[part_shape] * 4,
        scratch_shapes=[flat_rows, flat_rows, held_f],
        compiler_params=params(),
        name="end_states",
    )(document_starts, base, key_rows, value_rows)

    entering = pair_scan(list(states), False, shard, shards, keeps, shards // 2 - 1)

    query_major, key_major, value_major, grad_major = pl.pallas_call(
        turn_kernel,
        grid=grid,
        in_specs=[SMEM] + [native] * 4,
        out_specs=[major] * 4,
        out_shape=[major_shape] * 4,
        scratch_shapes=[flat_rows] * 4,
        compiler_params=params(),
        name="head_major",
    )(base, queries, key_rows, value_rows, grad_normed)

    attended, entry = pl.pallas_call(
        local_kernel,
        grid=grid,
        in_specs=[SMEM, SMEM, major, major, major],
        out_specs=[major, pl.BlockSpec((1, heads, width, width), lambda c: (c, 0, 0, 0))],
        out_shape=[
            jax.ShapeDtypeStruct((heads, rows, width), F32),
            jax.ShapeDtypeStruct((steps, heads, width, width), BF16),
        ],
        scratch_shapes=[held_f, mask_bf, token_bf, token_bf],
        compiler_params=params(),
        name="local_attention",
    )(document_starts, base, query_major, key_major, value_major)

    sums = pl.pallas_call(
        sums_kernel,
        grid=grid,
        in_specs=[SMEM, SMEM, major, major, major, gain_spec] + [state_part] * 4,
        out_specs=sums_spec,
        out_shape=jax.ShapeDtypeStruct((sum_rows, LANES), F32),
        scratch_shapes=[held_bf, token_f, token_f, token_bf],
        compiler_params=params(),
        name="token_sums",
    )(document_starts, base, query_major, attended, grad_major, norm_gain, *entering)
    sums = lax.psum(sums, "head")

    exits = pl.pallas_call(
        functools.partial(exit_kernel, features),
        grid=grid,
        in_specs=[SMEM, SMEM, major, major, major, gain_spec, sums_spec] + [state_part] * 4,
        out_specs=[state_part] * 4,
        out_shape=[part_shape] * 4,
        scratch_shapes=[held_bf, token_f, token_f, token_bf, held_f],
        compiler_params=params(),
        name="start_grads",
    )(document_starts, base, query_major, attended, grad_major, norm_gain, sums, *entering)

    leaving = pair_scan(list(exits), True, shard, shards, keeps, shards // 2 - 1)

    normed, grad_queries, grad_att, gain_sum = pl.pallas_call(
        functools.partial(query_kernel, features),
        grid=grid,
        in_specs=[SMEM, SMEM]
        + [major] * 5
        + [pl.BlockSpec((1, heads, width, width), lambda c: (c, 0, 0, 0)), gain_spec, sums_spec]
        + [state_part] * 4,
        out_specs=[native, native, major, gain_spec],
        out_shape=[native_shape, native_shape, major_shape, jax.ShapeDtypeStruct((heads, width), F32)],
        scratch_shapes=[
            held_f, token_f, token_f, token_f, token_bf, mask_bf, flat_rows, flat_rows,
            pltpu.VMEM((heads, width), F32),
        ],
        compiler_params=params(),
        name="query_grads",
    )(
        document_starts, base, query_major, key_major, value_major, attended, grad_major, entry,
        norm_gain, sums, *entering,
    )
    grad_gain = sum_over(gain_sum, "ctx") / math.sqrt(rows * shards)

    key_local, value_local = pl.pallas_call(
        key_kernel,
        grid=grid,
        in_specs=[SMEM, SMEM] + [major_back] * 4,
        out_specs=[major_back] * 2,
        out_shape=[major_shape] * 2,
        scratch_shapes=[held_f, mask_bf, token_bf, token_bf],
        compiler_params=params(),
        name="local_key_grads",
    )(document_starts, base, query_major, key_major, value_major, grad_att)

    grad_keys, grad_values = pl.pallas_call(
        last_kernel,
        grid=grid,
        in_specs=[SMEM, SMEM] + [major] * 4 + [state_part] * 4,
        out_specs=[native] * 2,
        out_shape=[native_shape] * 2,
        scratch_shapes=[held_bf, token_bf, flat_rows, flat_rows],
        compiler_params=params(),
        name="key_grads",
    )(document_starts, base, key_major, value_major, key_local, value_local, *leaving)
    return normed, grad_queries, grad_keys, grad_values, grad_gain


def solution(mesh):
    tokens = P("ctx", "head", None)
    in_specs = (tokens, tokens, tokens, tokens, P("head", None), P())
    out_specs = (tokens, tokens, tokens, tokens, P("head", None))
    return jax.shard_map(local, mesh=mesh, in_specs=in_specs, out_specs=out_specs, check_vma=False)
```

time: 368 us -> 289 us (0.79)
  Pallas kernels: 0 us -> 155 us
  matrix products: 108 us -> 0 us
  waiting for transfers between devices: 119 us -> 52.2 us
  starting transfers between devices: 0.29 us -> 55.8 us
  local copies, waits for them, and re-layouts: 42.4 us -> 2.27 us
  other arithmetic: 45.8 us -> 14.3 us
  blocking collectives: 33 us -> 6.45 us
  between operations: 15.8 us -> 2.12 us
    pallas_call x0 -> x8, Pallas kernels: none -> 155 us  [the longest x1 35 us: local(): pl.pallas_call(functools.partial(query_kernel, features), grid=grid, in_s...]
    all_gather x2 -> x0, waiting for transfers between devices: 118 us -> none  [the longest x1 84.9 us: local(): gathered = lax.all_gather(running[None], 'ctx', axis=0, tiled=True)]
    dot_general x12 -> x0, matrix products: 108 us -> none  [the longest x1 14.9 us: local(): jnp.einsum('chts,cshd->cthd', grad_scores, tiled_key, preferred_element_t...]
    ppermute x0 -> x23, starting transfers between devices: none -> 55.8 us  [the longest x12 35.5 us: pair_scan(): incoming = lax.ppermute(running, 'ctx', step)]
    ppermute x0 -> x23, waiting for transfers between devices: none -> 52.2 us  [the longest x12 31.6 us: pair_scan(): incoming = lax.ppermute(running, 'ctx', step)]
    psum x3 -> x1, blocking collectives: 33 us -> 6.45 us  [local(): sums = lax.psum(sums, 'head')]
    convert_element_type x4 -> x0, local copies, waits for them, and re-layouts: 25.6 us -> none  [the longest x1 7.05 us: local(): grad_values = (value_intra + leave_col * value_inter).astype(jnp.bfloat16)]
    reduce_sum x5 -> x0, other arithmetic: 20.3 us -> none  [the longest x1 9.28 us: local(): gain_local = jnp.sum(upstream * scaled, axis=(0, 1))]
  transfers between devices with their start and end apart: 2 -> 23, of which waited for: 2 -> 16; matrix products, arithmetic and copies ran while one was open for 31% -> 5% of each run, Pallas kernels for 0% -> 37%
where the time goes in v1:
time: 289 us; the launch traced here: 288 us
  Pallas kernels  155 us (54%)
  starting transfers between devices  55.8 us (19%)
  waiting for transfers between devices  52.2 us (18%)
  other arithmetic  14.3 us (5%)
  blocking collectives  6.45 us (2%)
    ppermute x12, starting transfers between devices, pair_scan(): incoming = lax.ppermute(running, 'ctx', step)  35.5 us
    pallas_call x1, Pallas kernels, local(): pl.pallas_call(functools.partial(query_kernel, features), grid=grid, in_s...  35 us
    ppermute x12, waiting for transfers between devices, pair_scan(): incoming = lax.ppermute(running, 'ctx', step)  31.6 us
    pallas_call x1, Pallas kernels, local(): pl.pallas_call(turn_kernel, grid=grid, in_specs=[SMEM] + [native] * 4, ou...  24.6 us
    pallas_call x1, Pallas kernels, local(): pl.pallas_call(key_kernel, grid=grid, in_specs=[SMEM, SMEM] + [major_back...  24.2 us
    pallas_call x1, Pallas kernels, local(): pl.pallas_call(local_kernel, grid=grid, in_specs=[SMEM, SMEM, major, majo...  21.9 us
    pallas_call x1, Pallas kernels, local(): pl.pallas_call(last_kernel, grid=grid, in_specs=[SMEM, SMEM] + [major] *...  18.3 us
    ppermute x4, waiting for transfers between devices, pair_scan(): arrived = [lax.ppermute(p, 'ctx', swap) for p in parts[half:]]  15.6 us
  transfers between devices with their start and end apart: 23, of which 16 were waited for; matrix products, arithmetic and copies ran while one was open for 5% of the time, Pallas kernels for 37%

profile of v1, /device:TPU:0, one launch (start us, length us, event | category | flops | bytes accessed | tf_op | source)
XLA Modules:
  0.0 287.9 jit_solution(12468277164974009608)
XLA Ops:
  1.3 12.7 %end_states.1 = (f32[4,128,128]{2,1,0:T(8,128)}, f32[4,128,128]{2,1,0:T(8,128)}, f32[4,128,128]{2,1,0:T(8,128)}, f32[4,128,128]{2,1,0:T(8,128)}) custom-call(s32[6]{0:T(128)} %starts.13, s32[2]{0:T(128)} %pad_add_fusion.base, bf16[1024,16,128]{2,1,0:T(8,128)(2,1)} %k_ref.1, bf16[1024,16,128]{2,1,0:T(8,128)(2,1)} %v_ref.1), custom_call_target="tpu_custom_call" | custom-call | tf_op jit(solution)/shard_map/end_states/pallas_call | solution.py:442
  16.9 6.4 %collective-permute-done = f32[4,128,128]{2,1,0:T(8,128)S(1)} collective-permute-done((f32[4,128,128]{2,1,0:T(8,128)}, f32[4,128,128]{2,1,0:T(8,128)S(1)}, u32[]{:S(2)}, u32[]{:S(2)}) %collective-permute-start) | collective-permute-done | bytes 262176 | tf_op jit(solution)/shard_map/ppermute | solution.py:383
  25.0 7.1 %collective-permute-start.1 = (f32[4,128,128]{2,1,0:T(8,128)S(1)}, f32[4,128,128]{2,1,0:T(8,128)S(1)}, u32[]{:S(2)}, u32[]{:S(2)}) collective-permute-start(f32[4,128,128]{2,1,0:T(8,128)S(1)} %multiply_add_fusion.15), channel_id=1, source_target_pairs={{0,8},{4,12},{8,16},{12,20},{16,24},{20,28},{1,9},{5,13},{9,17},{1... | collective-permute-start | bytes 786440 | tf_op jit(solution)/shard_map/ppermute | solution.py:391
  33.7 4.0 %collective-permute-start.5 = (f32[4,128,128]{2,1,0:T(8,128)S(1)}, f32[4,128,128]{2,1,0:T(8,128)S(1)}, u32[]{:S(2)}, u32[]{:S(2)}) collective-permute-start(f32[4,128,128]{2,1,0:T(8,128)S(1)} %multiply_add_fusion.11), channel_id=1, source_target_pairs={{0,8},{4,12},{8,16},{12,20},{16,24},{20,28},{1,9},{5,13},{9,17},{1... | collective-permute-start | bytes 786440 | tf_op jit(solution)/shard_map/ppermute | solution.py:391
  39.0 3.5 %collective-permute-start.2 = (f32[4,128,128]{2,1,0:T(8,128)S(1)}, f32[4,128,128]{2,1,0:T(8,128)S(1)}, u32[]{:S(2)}, u32[]{:S(2)}) collective-permute-start(f32[4,128,128]{2,1,0:T(8,128)S(1)} %multiply_add_fusion.14), channel_id=1, source_target_pairs={{0,8},{4,12},{8,16},{12,20},{16,24},{20,28},{1,9},{5,13},{9,17},{1... | collective-permute-start | bytes 786440 | tf_op jit(solution)/shard_map/ppermute | solution.py:391
  43.0 4.4 %collective-permute-start.6 = (f32[4,128,128]{2,1,0:T(8,128)S(1)}, f32[4,128,128]{2,1,0:T(8,128)S(1)}, u32[]{:S(2)}, u32[]{:S(2)}) collective-permute-start(f32[4,128,128]{2,1,0:T(8,128)S(1)} %multiply_add_fusion.10), channel_id=1, source_target_pairs={{0,8},{4,12},{8,16},{12,20},{16,24},{20,28},{1,9},{5,13},{9,17},{1... | collective-permute-start | bytes 786440 | tf_op jit(solution)/shard_map/ppermute | solution.py:391
  49.3 4.4 %collective-permute-start.3 = (f32[4,128,128]{2,1,0:T(8,128)S(1)}, f32[4,128,128]{2,1,0:T(8,128)S(1)}, u32[]{:S(2)}, u32[]{:S(2)}) collective-permute-start(f32[4,128,128]{2,1,0:T(8,128)S(1)} %multiply_add_fusion.13), channel_id=1, source_target_pairs={{0,8},{4,12},{8,16},{12,20},{16,24},{20,28},{1,9},{5,13},{9,17},{1... | collective-permute-start | bytes 786440 | tf_op jit(solution)/shard_map/ppermute | solution.py:391
  54.9 4.4 %collective-permute-start.7 = (f32[4,128,128]{2,1,0:T(8,128)S(1)}, f32[4,128,128]{2,1,0:T(8,128)S(1)}, u32[]{:S(2)}, u32[]{:S(2)}) collective-permute-start(f32[4,128,128]{2,1,0:T(8,128)S(1)} %multiply_add_fusion.9), channel_id=1, source_target_pairs={{0,8},{4,12},{8,16},{12,20},{16,24},{20,28},{1,9},{5,13},{9,17},{1... | collective-permute-start | bytes 786440 | tf_op jit(solution)/shard_map/ppermute | solution.py:391
  67.4 24.6 %head_major.1 = (bf16[16,1024,128]{2,1,0:T(8,128)(2,1)}, bf16[16,1024,128]{2,1,0:T(8,128)(2,1)}, bf16[16,1024,128]{2,1,0:T(8,128)(2,1)}, bf16[16,1024,128]{2,1,0:T(8,128)(2,1)}) custom-call(s32[2]{0:T(128)} %pad_add_fusion.base, bf16[1024,16,128]{2,1,0:T(8,128)(2,1)} %refs_0_.1, bf16[1024,16,128]{2,1,0:T(8,128)(2,1)} %k_ref.1, bf16[1024,16,128]{2,1,0:T(8,128)(2,1)} %v_ref.1, ...), custom_call_target="tpu_custom_call" | custom-call | tf_op jit(solution)/shard_map/head_major/pallas_call | solution.py:455
  92.0 21.9 %local_attention.1 = (f32[16,1024,128]{2,1,0:T(8,128)}, bf16[4,16,128,128]{3,2,1,0:T(8,128)(2,1)}) custom-call(s32[6]{0:T(128)} %starts.13, s32[2]{0:T(128)} %pad_add_fusion.base, bf16[16,1024,128]{2,1,0:T(8,128)(2,1)} %get-tuple-element.27.q_ref, bf16[16,1024,128]{2,1,0:T(8,128)(2,1)} %get-tuple-element.28.k_ref, bf16[16,1024,128]{2,1,0:T(8,128)(2,1)} %get-tuple-element.29.v_ref), custom_call_target="tpu_custom_call" | custom-call | tf_op jit(solution)/shard_map/local_attention/pallas_call | solution.py:466
  114.8 10.6 %token_sums.1 = f32[16,128]{1,0:T(8,128)} custom-call(s32[6]{0:T(128)} %starts.13, s32[2]{0:T(128)} %pad_add_fusion.base, bf16[16,1024,128]{2,1,0:T(8,128)(2,1)} %get-tuple-element.27.q_ref, f32[16,1024,128]{2,1,0:T(8,128)} %get-tuple-element.30.att_ref, bf16[16,1024,128]{2,1,0:T(8,128)(2,1)} %get-tuple-element.31.g_ref, f32[16,128]{1,0:T(8,128)} %gain.5, ...), custom_call_target="tpu_custom_call" | custom-call | tf_op jit(solution)/shard_map/token_sums/pallas_call | solution.py:480
  125.4 6.4 %psum.7.sums = f32[16,128]{1,0:T(8,128)} all-reduce(f32[16,128]{1,0:T(8,128)} %token_sums.1), channel_id=1, replica_groups=mesh['ctx'=8,'head'=4] {'head'}, use_global_device_ids=true, to_apply=%region_1.2 | all-reduce | flops 2048 | bytes 16384 | tf_op jit(solution)/shard_map/psum | solution.py:490
  131.9 7.4 %start_grads.1 = (f32[4,128,128]{2,1,0:T(8,128)}, f32[4,128,128]{2,1,0:T(8,128)}, f32[4,128,128]{2,1,0:T(8,128)}, f32[4,128,128]{2,1,0:T(8,128)}) custom-call(s32[6]{0:T(128)} %starts.13, s32[2]{0:T(128)} %pad_add_fusion.base, bf16[16,1024,128]{2,1,0:T(8,128)(2,1)} %get-tuple-element.27.q_ref, f32[16,1024,128]{2,1,0:T(8,128)} %get-tuple-element.30.att_ref, ...), custom_call_target="tpu_custom_call" | custom-call | tf_op jit(solution)/shard_map/start_grads/pallas_call | solution.py:492
  139.3 5.9 %collective-permute-start.14 = (f32[4,128,128]{2,1,0:T(8,128)}, f32[4,128,128]{2,1,0:T(8,128)S(1)}, u32[]{:S(2)}, u32[]{:S(2)}) collective-permute-start(f32[4,128,128]{2,1,0:T(8,128)} %get-tuple-element.44), channel_id=1, source_target_pairs={{0,4},{4,0},{8,12},{12,8},{16,20},{20,16},{24,28},{28,24},{1,5},{5... | collective-permute-start | bytes 786440 | tf_op jit(solution)/shard_map/ppermute | solution.py:383
  145.3 7.3 %collective-permute-done.14 = f32[4,128,128]{2,1,0:T(8,128)S(1)} collective-permute-done((f32[4,128,128]{2,1,0:T(8,128)}, f32[4,128,128]{2,1,0:T(8,128)S(1)}, u32[]{:S(2)}, u32[]{:S(2)}) %collective-permute-start.14) | collective-permute-done | bytes 262176 | tf_op jit(solution)/shard_map/ppermute | solution.py:383
  160.3 6.2 %collective-permute-done.15 = f32[4,128,128]{2,1,0:T(8,128)S(1)} collective-permute-done((f32[4,128,128]{2,1,0:T(8,128)S(1)}, f32[4,128,128]{2,1,0:T(8,128)S(1)}, u32[]{:S(2)}, u32[]{:S(2)}) %collective-permute-start.15) | collective-permute-done | bytes 262176 | tf_op jit(solution)/shard_map/ppermute | solution.py:391
  167.8 5.7 %collective-permute-done.11 = f32[4,128,128]{2,1,0:T(8,128)S(1)} collective-permute-done((f32[4,128,128]{2,1,0:T(8,128)S(1)}, f32[4,128,128]{2,1,0:T(8,128)S(1)}, u32[]{:S(2)}, u32[]{:S(2)}) %collective-permute-start.11) | collective-permute-done | bytes 262176 | tf_op jit(solution)/shard_map/ppermute | solution.py:391
  174.9 4.3 %collective-permute-done.16 = f32[4,128,128]{2,1,0:T(8,128)S(1)} collective-permute-done((f32[4,128,128]{2,1,0:T(8,128)S(1)}, f32[4,128,128]{2,1,0:T(8,128)S(1)}, u32[]{:S(2)}, u32[]{:S(2)}) %collective-permute-start.16) | collective-permute-done | bytes 262176 | tf_op jit(solution)/shard_map/ppermute | solution.py:391
  180.5 4.4 %collective-permute-done.12 = f32[4,128,128]{2,1,0:T(8,128)S(1)} collective-permute-done((f32[4,128,128]{2,1,0:T(8,128)S(1)}, f32[4,128,128]{2,1,0:T(8,128)S(1)}, u32[]{:S(2)}, u32[]{:S(2)}) %collective-permute-start.12) | collective-permute-done | bytes 262176 | tf_op jit(solution)/shard_map/ppermute | solution.py:391
  186.2 4.3 %collective-permute-done.17 = f32[4,128,128]{2,1,0:T(8,128)S(1)} collective-permute-done((f32[4,128,128]{2,1,0:T(8,128)S(1)}, f32[4,128,128]{2,1,0:T(8,128)S(1)}, u32[]{:S(2)}, u32[]{:S(2)}) %collective-permute-start.17) | collective-permute-done | bytes 262176 | tf_op jit(solution)/shard_map/ppermute | solution.py:391
  197.4 35.0 %query_grads.1 = (bf16[1024,16,128]{2,1,0:T(8,128)(2,1)}, bf16[1024,16,128]{2,1,0:T(8,128)(2,1)}, bf16[16,1024,128]{2,1,0:T(8,128)(2,1)}, f32[16,128]{1,0:T(8,128)}) custom-call(s32[6]{0:T(128)} %starts.13, s32[2]{0:T(128)} %pad_add_fusion.base, bf16[16,1024,128]{2,1,0:T(8,128)(2,1)} %get-tuple-element.27.q_ref, ...), custom_call_target="tpu_custom_call" | custom-call | tf_op jit(solution)/shard_map/query_grads/pallas_call | solution.py:505
  233.1 3.3 %collective-permute-done.20 = f32[16,128]{1,0:T(8,128)S(1)} collective-permute-done((f32[16,128]{1,0:T(8,128)}, f32[16,128]{1,0:T(8,128)S(1)}, u32[]{:S(2)}, u32[]{:S(2)}) %collective-permute-start.20) | collective-permute-done | bytes 8224 | tf_op jit(solution)/shard_map/ppermute | solution.py:407
  244.0 24.2 %local_key_grads.1 = (bf16[16,1024,128]{2,1,0:T(8,128)(2,1)}, bf16[16,1024,128]{2,1,0:T(8,128)(2,1)}) custom-call(s32[6]{0:T(128)} %starts.13, s32[2]{0:T(128)} %pad_add_fusion.base, bf16[16,1024,128]{2,1,0:T(8,128)(2,1)} %get-tuple-element.27.q_ref, bf16[16,1024,128]{2,1,0:T(8,128)(2,1)} %get-tuple-element.28.k_ref, ...), custom_call_target="tpu_custom_call" | custom-call | tf_op jit(solution)/shard_map/local_key_grads/pallas_call | solution.py:526
  269.6 18.3 %key_grads.1 = (bf16[1024,16,128]{2,1,0:T(8,128)(2,1)}, bf16[1024,16,128]{2,1,0:T(8,128)(2,1)}) custom-call(s32[6]{0:T(128)} %starts.13, s32[2]{0:T(128)} %pad_add_fusion.base, bf16[16,1024,128]{2,1,0:T(8,128)(2,1)} %get-tuple-element.28.k_ref, bf16[16,1024,128]{2,1,0:T(8,128)(2,1)} %get-tuple-element.29.v_ref, ...), custom_call_target="tpu_custom_call" | custom-call | tf_op jit(solution)/shard_map/key_grads/pallas_call | solution.py:537
  (73 shorter events, 49.0 us)
Async XLA Ops:
  14.0 9.4 %collective-permute-start = (f32[4,128,128]{2,1,0:T(8,128)}, f32[4,128,128]{2,1,0:T(8,128)S(1)}, u32[]{:S(2)}, u32[]{:S(2)}) collective-permute-start(f32[4,128,128]{2,1,0:T(8,128)} %get-tuple-element.33), channel_id=1, source_target_pairs={{0,4},{4,0},{8,12},{12,8},{16,20},{20,16},{24,28},{28,24},{1,5},{5... | collective-permute-start | bytes 786440 | tf_op jit(solution)/shard_map/ppermute | solution.py:383
  15.0 17.1 %collective-permute-start.4 = (f32[4,128,128]{2,1,0:T(8,128)}, f32[4,128,128]{2,1,0:T(8,128)S(1)}, u32[]{:S(2)}, u32[]{:S(2)}) collective-permute-start(f32[4,128,128]{2,1,0:T(8,128)} %get-tuple-element.35), channel_id=1, source_target_pairs={{0,4},{4,0},{8,12},{12,8},{16,20},{20,16},{24,28},{28,24},{1,5},{5... | collective-permute-start | bytes 786440 | tf_op jit(solution)/shard_map/ppermute | solution.py:383
  25.0 14.0 %collective-permute-start.1 = (f32[4,128,128]{2,1,0:T(8,128)S(1)}, f32[4,128,128]{2,1,0:T(8,128)S(1)}, u32[]{:S(2)}, u32[]{:S(2)}) collective-permute-start(f32[4,128,128]{2,1,0:T(8,128)S(1)} %multiply_add_fusion.15), channel_id=1, source_target_pairs={{0,8},{4,12},{8,16},{12,20},{16,24},{20,28},{1,9},{5,13},{9,17},{1... | collective-permute-start | bytes 786440 | tf_op jit(solution)/shard_map/ppermute | solution.py:391
  33.7 9.3 %collective-permute-start.5 = (f32[4,128,128]{2,1,0:T(8,128)S(1)}, f32[4,128,128]{2,1,0:T(8,128)S(1)}, u32[]{:S(2)}, u32[]{:S(2)}) collective-permute-start(f32[4,128,128]{2,1,0:T(8,128)S(1)} %multiply_add_fusion.11), channel_id=1, source_target_pairs={{0,8},{4,12},{8,16},{12,20},{16,24},{20,28},{1,9},{5,13},{9,17},{1... | collective-permute-start | bytes 786440 | tf_op jit(solution)/shard_map/ppermute | solution.py:391
  39.0 10.2 %collective-permute-start.2 = (f32[4,128,128]{2,1,0:T(8,128)S(1)}, f32[4,128,128]{2,1,0:T(8,128)S(1)}, u32[]{:S(2)}, u32[]{:S(2)}) collective-permute-start(f32[4,128,128]{2,1,0:T(8,128)S(1)} %multiply_add_fusion.14), channel_id=1, source_target_pairs={{0,8},{4,12},{8,16},{12,20},{16,24},{20,28},{1,9},{5,13},{9,17},{1... | collective-permute-start | bytes 786440 | tf_op jit(solution)/shard_map/ppermute | solution.py:391
  43.0 11.8 %collective-permute-start.6 = (f32[4,128,128]{2,1,0:T(8,128)S(1)}, f32[4,128,128]{2,1,0:T(8,128)S(1)}, u32[]{:S(2)}, u32[]{:S(2)}) collective-permute-start(f32[4,128,128]{2,1,0:T(8,128)S(1)} %multiply_add_fusion.10), channel_id=1, source_target_pairs={{0,8},{4,12},{8,16},{12,20},{16,24},{20,28},{1,9},{5,13},{9,17},{1... | collective-permute-start | bytes 786440 | tf_op jit(solution)/shard_map/ppermute | solution.py:391
  49.3 11.2 %collective-permute-start.3 = (f32[4,128,128]{2,1,0:T(8,128)S(1)}, f32[4,128,128]{2,1,0:T(8,128)S(1)}, u32[]{:S(2)}, u32[]{:S(2)}) collective-permute-start(f32[4,128,128]{2,1,0:T(8,128)S(1)} %multiply_add_fusion.13), channel_id=1, source_target_pairs={{0,8},{4,12},{8,16},{12,20},{16,24},{20,28},{1,9},{5,13},{9,17},{1... | collective-permute-start | bytes 786440 | tf_op jit(solution)/shard_map/ppermute | solution.py:391
  54.9 9.4 %collective-permute-start.7 = (f32[4,128,128]{2,1,0:T(8,128)S(1)}, f32[4,128,128]{2,1,0:T(8,128)S(1)}, u32[]{:S(2)}, u32[]{:S(2)}) collective-permute-start(f32[4,128,128]{2,1,0:T(8,128)S(1)} %multiply_add_fusion.9), channel_id=1, source_target_pairs={{0,8},{4,12},{8,16},{12,20},{16,24},{20,28},{1,9},{5,13},{9,17},{1... | collective-permute-start | bytes 786440 | tf_op jit(solution)/shard_map/ppermute | solution.py:391
  61.8 52.1 %collective-permute-start.8 = (f32[4,128,128]{2,1,0:T(8,128)S(1)}, f32[4,128,128]{2,1,0:T(8,128)S(1)}, u32[]{:S(2)}, u32[]{:S(2)}) collective-permute-start(f32[4,128,128]{2,1,0:T(8,128)S(1)} %get-tuple-element.55), channel_id=1, source_target_pairs={{0,4},{4,0},{8,12},{12,8},{16,20},{20,16},{24,28},{28,24},{1,5},{5... | collective-permute-start | bytes 786440 | tf_op jit(solution)/shard_map/ppermute | solution.py:397
  65.7 48.3 %collective-permute-start.9 = (f32[4,128,128]{2,1,0:T(8,128)S(1)}, f32[4,128,128]{2,1,0:T(8,128)S(1)}, u32[]{:S(2)}, u32[]{:S(2)}) collective-permute-start(f32[4,128,128]{2,1,0:T(8,128)S(1)} %get-tuple-element.53), channel_id=1, source_target_pairs={{0,4},{4,0},{8,12},{12,8},{16,20},{20,16},{24,28},{28,24},{1,5},{5... | collective-permute-start | bytes 786440 | tf_op jit(solution)/shard_map/ppermute | solution.py:397
  139.3 55.3 %copy-start.4 = (f32[4,128,128]{2,1,0:T(8,128)S(1)}, f32[4,128,128]{2,1,0:T(8,128)}, u32[]{:S(2)}) copy-start(f32[4,128,128]{2,1,0:T(8,128)} %get-tuple-element.43) | copy-start | bytes 786436
  139.3 13.2 %collective-permute-start.14 = (f32[4,128,128]{2,1,0:T(8,128)}, f32[4,128,128]{2,1,0:T(8,128)S(1)}, u32[]{:S(2)}, u32[]{:S(2)}) collective-permute-start(f32[4,128,128]{2,1,0:T(8,128)} %get-tuple-element.44), channel_id=1, source_target_pairs={{0,4},{4,0},{8,12},{12,8},{16,20},{20,16},{24,28},{28,24},{1,5},{5... | collective-permute-start | bytes 786440 | tf_op jit(solution)/shard_map/ppermute | solution.py:383
  145.2 12.2 %collective-permute-start.10 = (f32[4,128,128]{2,1,0:T(8,128)}, f32[4,128,128]{2,1,0:T(8,128)S(1)}, u32[]{:S(2)}, u32[]{:S(2)}) collective-permute-start(f32[4,128,128]{2,1,0:T(8,128)} %get-tuple-element.42), channel_id=1, source_target_pairs={{0,4},{4,0},{8,12},{12,8},{16,20},{20,16},{24,28},{28,24},{1,5},{5... | collective-permute-start | bytes 786440 | tf_op jit(solution)/shard_map/ppermute | solution.py:383
  154.1 12.3 %collective-permute-start.15 = (f32[4,128,128]{2,1,0:T(8,128)S(1)}, f32[4,128,128]{2,1,0:T(8,128)S(1)}, u32[]{:S(2)}, u32[]{:S(2)}) collective-permute-start(f32[4,128,128]{2,1,0:T(8,128)S(1)} %multiply_add_fusion.3), channel_id=1, source_target_pairs={{8,0},{12,4},{16,8},{20,12},{24,16},{28,20},{9,1},{13,5},{17,9},{2... | collective-permute-start | bytes 786440 | tf_op jit(solution)/shard_map/ppermute | solution.py:391
  159.0 14.6 %collective-permute-start.11 = (f32[4,128,128]{2,1,0:T(8,128)S(1)}, f32[4,128,128]{2,1,0:T(8,128)S(1)}, u32[]{:S(2)}, u32[]{:S(2)}) collective-permute-start(f32[4,128,128]{2,1,0:T(8,128)S(1)} %multiply_add_fusion.7), channel_id=1, source_target_pairs={{8,0},{12,4},{16,8},{20,12},{24,16},{28,20},{9,1},{13,5},{17,9},{2... | collective-permute-start | bytes 786440 | tf_op jit(solution)/shard_map/ppermute | solution.py:391
  166.5 12.7 %collective-permute-start.16 = (f32[4,128,128]{2,1,0:T(8,128)S(1)}, f32[4,128,128]{2,1,0:T(8,128)S(1)}, u32[]{:S(2)}, u32[]{:S(2)}) collective-permute-start(f32[4,128,128]{2,1,0:T(8,128)S(1)} %multiply_add_fusion.2), channel_id=1, source_target_pairs={{8,0},{12,4},{16,8},{20,12},{24,16},{28,20},{9,1},{13,5},{17,9},{2... | collective-permute-start | bytes 786440 | tf_op jit(solution)/shard_map/ppermute | solution.py:391
  173.6 11.3 %collective-permute-start.12 = (f32[4,128,128]{2,1,0:T(8,128)S(1)}, f32[4,128,128]{2,1,0:T(8,128)S(1)}, u32[]{:S(2)}, u32[]{:S(2)}) collective-permute-start(f32[4,128,128]{2,1,0:T(8,128)S(1)} %multiply_add_fusion.6), channel_id=1, source_target_pairs={{8,0},{12,4},{16,8},{20,12},{24,16},{28,20},{9,1},{13,5},{17,9},{2... | collective-permute-start | bytes 786440 | tf_op jit(solution)/shard_map/ppermute | solution.py:391
  179.2 11.3 %collective-permute-start.17 = (f32[4,128,128]{2,1,0:T(8,128)S(1)}, f32[4,128,128]{2,1,0:T(8,128)S(1)}, u32[]{:S(2)}, u32[]{:S(2)}) collective-permute-start(f32[4,128,128]{2,1,0:T(8,128)S(1)} %multiply_add_fusion.1), channel_id=1, source_target_pairs={{8,0},{12,4},{16,8},{20,12},{24,16},{28,20},{9,1},{13,5},{17,9},{2... | collective-permute-start | bytes 786440 | tf_op jit(solution)/shard_map/ppermute | solution.py:391
  184.9 9.7 %collective-permute-start.13 = (f32[4,128,128]{2,1,0:T(8,128)S(1)}, f32[4,128,128]{2,1,0:T(8,128)S(1)}, u32[]{:S(2)}, u32[]{:S(2)}) collective-permute-start(f32[4,128,128]{2,1,0:T(8,128)S(1)} %multiply_add_fusion.5), channel_id=1, source_target_pairs={{8,0},{12,4},{16,8},{20,12},{24,16},{28,20},{9,1},{13,5},{17,9},{2... | collective-permute-start | bytes 786440 | tf_op jit(solution)/shard_map/ppermute | solution.py:391
  191.9 77.0 %collective-permute-start.19 = (f32[4,128,128]{2,1,0:T(8,128)S(1)}, f32[4,128,128]{2,1,0:T(8,128)S(1)}, u32[]{:S(2)}, u32[]{:S(2)}) collective-permute-start(f32[4,128,128]{2,1,0:T(8,128)S(1)} %get-tuple-element.49), channel_id=1, source_target_pairs={{0,4},{4,0},{8,12},{12,8},{16,20},{20,16},{24,28},{28,24},{1,5},{5... | collective-permute-start | bytes 786440 | tf_op jit(solution)/shard_map/ppermute | solution.py:397
  195.9 72.9 %collective-permute-start.18 = (f32[4,128,128]{2,1,0:T(8,128)S(1)}, f32[4,128,128]{2,1,0:T(8,128)S(1)}, u32[]{:S(2)}, u32[]{:S(2)}) collective-permute-start(f32[4,128,128]{2,1,0:T(8,128)S(1)} %get-tuple-element.51), channel_id=1, source_target_pairs={{0,4},{4,0},{8,12},{12,8},{16,20},{20,16},{24,28},{28,24},{1,5},{5... | collective-permute-start | bytes 786440 | tf_op jit(solution)/shard_map/ppermute | solution.py:397
  232.4 3.9 %collective-permute-start.20 = (f32[16,128]{1,0:T(8,128)}, f32[16,128]{1,0:T(8,128)S(1)}, u32[]{:S(2)}, u32[]{:S(2)}) collective-permute-start(f32[16,128]{1,0:T(8,128)} %get-tuple-element.48), channel_id=1, source_target_pairs={{0,4},{4,0},{8,12},{12,8},{16,20},{20,16},{24,28},{28,24},{1,5},{5... | collective-permute-start | bytes 24584 | tf_op jit(solution)/shard_map/ppermute | solution.py:407
  237.1 3.7 %collective-permute-start.21 = (f32[16,128]{1,0:T(8,128)S(1)}, f32[16,128]{1,0:T(8,128)S(1)}, u32[]{:S(2)}, u32[]{:S(2)}) collective-permute-start(f32[16,128]{1,0:T(8,128)S(1)} %add.94), channel_id=1, source_target_pairs={{0,8},{4,12},{8,0},{12,4},{16,24},{20,28},{24,16},{28,20},{1,9},{5... | collective-permute-start | bytes 24584 | tf_op jit(solution)/shard_map/ppermute | solution.py:407
  240.7 27.5 %collective-permute-start.22 = (f32[16,128]{1,0:T(8,128)S(1)}, f32[16,128]{1,0:T(8,128)S(1)}, u32[]{:S(2)}, u32[]{:S(2)}) collective-permute-start(f32[16,128]{1,0:T(8,128)S(1)} %add.95), channel_id=1, source_target_pairs={{0,16},{4,20},{8,24},{12,28},{16,0},{20,4},{24,8},{28,12},{1,17},{... | collective-permute-start | bytes 24584 | tf_op jit(solution)/shard_map/ppermute | solution.py:407
  (8 other events, 165.8 us)
